TPU v7x, 32 devices: a whole 2x2x4 slice. The times are simulated.
32 devices in a mesh: seq: 8 (over y, x, core), chan: 4 (over z).
Axes of the slice: x: 2, y: 2, z: 4, core: 2. Of those that a mesh axis runs over, the one named last changes fastest.
Arguments:
- tokens: bfloat16 [768, 16384], P('chan', 'seq'), may hold values from -7.5 to 7.5
- filter_spectrum: float32 [2, 768, 16384], P(None, 'chan', 'seq'), may hold values from -6 to 6
- skip_weight: float32 [768], P('chan'), may hold values from -1 to 1
- norm_gain: float32 [768], P('chan'), may hold values from 0.5 to 1.5
- mlp_gain: float32 [768], P('chan'), may hold values from 0.5 to 1.5
- mix_in: bfloat16 [4, 36864], P('chan'), may hold values from -0.4375 to 0.4375
- up_weight: bfloat16 [4, 147456], P('chan'), may hold values from -0.4375 to 0.4375
- down_weight: bfloat16 [4, 147456], P('chan'), may hold values from -0.21875 to 0.21875
- mix_out: bfloat16 [4, 36864], P('chan'), may hold values from -0.4375 to 0.4375
Outputs:
- mixed: bfloat16 [768, 16384], P('chan', 'seq')
All inputs are finite; a program needn't handle non-finite values.
Results may differ from a plain program's by a relative error of at most 0.013.
Values may be sent and summed in bfloat16 or wider, within the bound.
A program may use at most 64 MiB of HBM per device.

v0:
```python
import functools
import math

import jax
import jax.numpy as jnp
import numpy as np
from jax import lax
from jax.experimental import pallas as pl
from jax.experimental.pallas import tpu as pltpu
from jax.sharding import PartitionSpec as P

RADIX = 64


def dft_tables(length_dft):
    position = jnp.arange(length_dft, dtype=jnp.int32)
    phase_int = position[:, None] * position[None, :] % length_dft
    radians = phase_int.astype(jnp.float32) * (2.0 * math.pi / length_dft)
    return (jnp.cos(radians).astype(jnp.bfloat16), jnp.sin(radians).astype(jnp.bfloat16))


def twiddle_tables(wide, narrow):
    outer_idx = jnp.arange(wide, dtype=jnp.int32)
    inner_idx = jnp.arange(narrow, dtype=jnp.int32)
    phase_int = outer_idx[:, None] * inner_idx[None, :] % (wide * narrow)
    radians = phase_int.astype(jnp.float32) * (2.0 * math.pi / (wide * narrow))
    return (jnp.cos(radians)[None], jnp.sin(radians)[None])


def mix_form(form, left_op, right_op):
    return jnp.einsum(form, left_op.astype(jnp.float32), right_op.astype(jnp.float32))


def forward_local(values, tables):
    cos_w, sin_w, cos_a, sin_a = tables
    rows_all, length_dft = values.shape
    wide = cos_w.shape[0]
    narrow = length_dft // wide
    grid = values.reshape(rows_all, wide, narrow)
    section_re = mix_form("rba,bk->rka", grid, cos_w)
    section_im = -mix_form("rba,bk->rka", grid, sin_w)
    twid_cos, twid_sin = twiddle_tables(wide, narrow)
    inner_re = (section_re * twid_cos + section_im * twid_sin).astype(jnp.bfloat16)
    inner_im = (section_im * twid_cos - section_re * twid_sin).astype(jnp.bfloat16)
    out_re = mix_form("rka,ad->rdk", inner_re, cos_a) + mix_form("rka,ad->rdk", inner_im, sin_a)
    out_im = mix_form("rka,ad->rdk", inner_im, cos_a) - mix_form("rka,ad->rdk", inner_re, sin_a)
    return (out_re.reshape(rows_all, length_dft), out_im.reshape(rows_all, length_dft))


def inverse_local(values_re, values_im, tables):
    cos_w, sin_w, cos_a, sin_a = tables
    rows_all, length_dft = values_re.shape
    wide = cos_w.shape[0]
    narrow = length_dft // wide
    grid_re = values_re.reshape(rows_all, narrow, wide)
    grid_im = values_im.reshape(rows_all, narrow, wide)
    back_re = mix_form("rdk,da->rka", grid_re, cos_a) - mix_form("rdk,da->rka", grid_im, sin_a)
    back_im = mix_form("rdk,da->rka", grid_im, cos_a) + mix_form("rdk,da->rka", grid_re, sin_a)
    twid_cos, twid_sin = twiddle_tables(wide, narrow)
    outer_re = (back_re * twid_cos - back_im * twid_sin).astype(jnp.bfloat16)
    outer_im = (back_im * twid_cos + back_re * twid_sin).astype(jnp.bfloat16)
    real_part = mix_form("rka,kb->rba", outer_re, cos_w) - mix_form("rka,kb->rba", outer_im, sin_w)
    return real_part.reshape(rows_all, length_dft)


def small_mix(table, values):
    return jnp.einsum("gp,cpr->cgr", table.astype(jnp.float32), values.astype(jnp.float32))


def spectral(normed, spectrum, tables, cos_p, sin_p, send_out, send_back):
    col_width, tok_rows = normed.shape
    groups = cos_p.shape[0]
    share = tok_rows // groups
    length_all = tok_rows * groups
    device_pos = lax.axis_index("seq")
    frequency = jnp.arange(tok_rows, dtype=jnp.int32)
    radians = (frequency * device_pos).astype(jnp.float32) * (2.0 * math.pi / length_all)
    twist_cos = jnp.cos(radians)[None, :]
    twist_sin = jnp.sin(radians)[None, :]
    first_re, first_im = forward_local(normed, tables)
    twisted_re = (first_re * twist_cos + first_im * twist_sin).astype(jnp.bfloat16)
    twisted_im = (first_im * twist_cos - first_re * twist_sin).astype(jnp.bfloat16)
    moved_re, moved_im = send_out((twisted_re, twisted_im))
    moved_re = moved_re.reshape(col_width, groups, share)
    moved_im = moved_im.reshape(col_width, groups, share)
    spec_re = small_mix(cos_p, moved_re) + small_mix(sin_p, moved_im)
    spec_im = small_mix(cos_p, moved_im) - small_mix(sin_p, moved_re)
    filter_re = spectrum[0].reshape(col_width, groups, share)
    filter_im = spectrum[1].reshape(col_width, groups, share)
    filtered_re = (filter_re * spec_re - filter_im * spec_im).astype(jnp.bfloat16)
    filtered_im = (filter_re * spec_im + filter_im * spec_re).astype(jnp.bfloat16)
    back_re = small_mix(cos_p, filtered_re) - small_mix(sin_p, filtered_im)
    back_im = small_mix(cos_p, filtered_im) + small_mix(sin_p, filtered_re)
    owned_freq = device_pos * share + jnp.arange(share, dtype=jnp.int32)
    devices = jnp.arange(groups, dtype=jnp.int32)
    undo_radians = (devices[:, None] * owned_freq[None, :]).astype(jnp.float32) * (
        2.0 * math.pi / length_all
    )
    undo_cos = jnp.cos(undo_radians)[None]
    undo_sin = jnp.sin(undo_radians)[None]
    turned_re = (
        (back_re * undo_cos - back_im * undo_sin).astype(jnp.bfloat16).reshape(col_width, tok_rows)
    )
    turned_im = (
        (back_im * undo_cos + back_re * undo_sin).astype(jnp.bfloat16).reshape(col_width, tok_rows)
    )
    home_re, home_im = send_back((turned_re, turned_im))
    return inverse_local(home_re, home_im, tables) * (1.0 / length_all)


MESH = pl.DeviceIdType.MESH
VMEM_BYTES = 56 * 1024 * 1024


def vmem_spec():
    return pl.BlockSpec(memory_space=pltpu.VMEM)


def greet(axis, n):
    me = lax.axis_index(axis)
    barrier = pltpu.get_barrier_semaphore()
    for k in range(1, n):
        pl.semaphore_signal(
            barrier, inc=1, device_id={axis: lax.rem(me + k, n)}, device_id_type=MESH
        )
    return barrier


def share_stats(n, barrier, stats, send_sem, recv_sem):
    me = lax.axis_index("chan")
    pl.semaphore_wait(barrier, n - 1)
    copies = []
    for k in range(1, n):
        copy = pltpu.make_async_remote_copy(
            src_ref=stats.at[0],
            dst_ref=stats.at[k],
            send_sem=send_sem.at[k],
            recv_sem=recv_sem.at[k],
            device_id={"chan": lax.rem(me + k, n)},
            device_id_type=MESH,
        )
        copy.start()
        copies.append(copy)
    for copy in copies:
        copy.wait()
    total = stats[0]
    for k in range(1, n):
        total = total + stats[k]
    return total


def norm_kernel(n, width, x_ref, gain_ref, out_ref, stats, send_sem, recv_sem):
    barrier = greet("chan", n)
    cols = x_ref.shape[1]
    step = min(cols, 512)
    for c in range(0, cols, step):
        x = x_ref[:, c : c + step].astype(jnp.float32)
        stats[0, 0:1, c : c + step] = jnp.sum(x, axis=0, keepdims=True)
        stats[0, 1:2, c : c + step] = jnp.sum(x * x, axis=0, keepdims=True)
    total = share_stats(n, barrier, stats, send_sem, recv_sem)
    mean = total[0:1] / width
    scale = lax.rsqrt(total[1:2] / width - mean * mean + 1e-05)
    gain = gain_ref[...]
    for c in range(0, cols, step):
        x = x_ref[:, c : c + step].astype(jnp.float32)
        y = (x - mean[:, c : c + step]) * scale[:, c : c + step] * gain
        out_ref[:, c : c + step] = y.astype(jnp.bfloat16)


def first_norm(n, width, tokens, gain):
    return pl.pallas_call(
        functools.partial(norm_kernel, n, width),
        out_shape=jax.ShapeDtypeStruct(tokens.shape, jnp.bfloat16),
        in_specs=[vmem_spec()] * 2,
        out_specs=vmem_spec(),
        scratch_shapes=[
            pltpu.VMEM((n, 2, tokens.shape[1]), jnp.float32),
            pltpu.SemaphoreType.DMA((n,)),
            pltpu.SemaphoreType.DMA((n,)),
        ],
        compiler_params=pltpu.CompilerParams(
            collective_id=0, has_side_effects=True, vmem_limit_bytes=VMEM_BYTES
        ),
    )(tokens, gain[:, None])


def small_dft(values, sign):
    n = len(values)
    if n == 1:
        return values
    even = small_dft(values[0::2], sign)
    odd = small_dft(values[1::2], sign)
    out = [None] * n
    for k in range(n // 2):
        re, im = odd[k]
        if k == 0:
            tr, ti = re, im
        elif 4 * k == n:
            tr, ti = (-im, re) if sign > 0 else (im, -re)
        else:
            c = float(np.float64(math.cos(2 * math.pi * k / n)).astype(jnp.bfloat16))
            s = sign * float(np.float64(math.sin(2 * math.pi * k / n)).astype(jnp.bfloat16))
            tr, ti = re * c - im * s, re * s + im * c
        er, ei = even[k]
        out[k] = (er + tr, ei + ti)
        out[k + n // 2] = (er - tr, ei - ti)
    return out


def conv_kernel(
    n, x_ref, filt_hbm, cos_hbm, sin_hbm, twc_ref, tws_ref, undo_c, undo_s, out_ref,
    cos_v, sin_v, filt_v, send_f, recv_f, send_b, recv_b,
    load_sem, filt_sem, sf_sem, rf_sem, sb_sem, rb_sem,
):
    me = lax.axis_index("seq")
    barrier = greet("seq", n)
    rows, cols = x_ref.shape
    share = cols // n
    parts = sb_sem.shape[1]
    group = rows // parts

    def block_of(k):
        return pl.ds(pl.multiple_of(lax.rem(me + k, n) * share, share), share)

    def load(k, which):
        hbm, vmem = ((cos_hbm, cos_v), (sin_hbm, sin_v))[which]
        view = block_of(k)
        return pltpu.make_async_copy(hbm.at[:, view], vmem.at[:, view], load_sem.at[k, which])

    filt_copy = pltpu.make_async_copy(filt_hbm, filt_v, filt_sem.at[0])
    for k in list(range(1, n)) + [0]:
        load(k, 0).start()
        load(k, 1).start()
    filt_copy.start()
    pl.semaphore_wait(barrier, n - 1)

    def transform(k):
        load(k, 0).wait()
        load(k, 1).wait()
        view = block_of(k)
        x = x_ref[...]
        re = jnp.dot(x, cos_v[:, view], preferred_element_type=jnp.float32)
        im = -jnp.dot(x, sin_v[:, view], preferred_element_type=jnp.float32)
        tc, ts = twc_ref[:, view], tws_ref[:, view]
        return (
            (re * tc + im * ts).astype(jnp.bfloat16),
            (im * tc - re * ts).astype(jnp.bfloat16),
        )

    def outward(k):
        peer = lax.rem(me + k, n)
        return pltpu.make_async_remote_copy(
            src_ref=send_f.at[k],
            dst_ref=recv_f.at[me],
            send_sem=sf_sem.at[k],
            recv_sem=rf_sem.at[k],
            device_id={"seq": peer},
            device_id_type=MESH,
        )

    def forward(k, carry):
        re, im = transform(k)
        send_f[k, 0] = re
        send_f[k, 1] = im
        outward(k).start()
        return carry

    lax.fori_loop(1, n, forward, 0)
    re, im = transform(0)
    recv_f[me, 0] = re
    recv_f[me, 1] = im
    filt_copy.wait()

    def arrive(k, carry):
        outward(k).wait()
        return carry

    lax.fori_loop(1, n, arrive, 0)

    def inward(k, part):
        peer = lax.rem(me + k, n)
        view = pl.ds(part * group, group)
        return pltpu.make_async_remote_copy(
            src_ref=send_b.at[peer, :, view],
            dst_ref=recv_b.at[k, :, view],
            send_sem=sb_sem.at[k, part],
            recv_sem=rb_sem.at[k, part],
            device_id={"seq": peer},
            device_id_type=MESH,
        )

    lanes = 128
    for part in range(parts):

        def middle(i, carry, part=part):
            view = pl.ds(pl.multiple_of(part * group + i * 16, 16), 16)
            for c in range(0, share, lanes):
                values = [
                    (
                        recv_f[p, 0, view, c : c + lanes].astype(jnp.float32),
                        recv_f[p, 1, view, c : c + lanes].astype(jnp.float32),
                    )
                    for p in range(n)
                ]
                spec = small_dft(values, -1)
                filtered = []
                for g in range(n):
                    sr, si = spec[g]
                    low = g * share + c
                    fr = filt_v[0, view, low : low + lanes]
                    fi = filt_v[1, view, low : low + lanes]
                    filtered.append((fr * sr - fi * si, fr * si + fi * sr))
                back = small_dft(filtered, 1)
                for p in range(n):
                    br, bi = back[p]
                    uc = undo_c[p : p + 1, c : c + lanes]
                    us = undo_s[p : p + 1, c : c + lanes]
                    send_b[p, 0, view, c : c + lanes] = (br * uc - bi * us).astype(jnp.bfloat16)
                    send_b[p, 1, view, c : c + lanes] = (bi * uc + br * us).astype(jnp.bfloat16)
            return carry

        lax.fori_loop(0, group // 16, middle, 0)

        def push(k, carry, part=part):
            inward(k, part).start()
            return carry

        lax.fori_loop(1, n, push, 0)

    tile = min(cols, 512)
    scale = 1.0 / (n * cols)

    def accumulate(re, im, source, first):
        view = pl.ds(pl.multiple_of(source * share, share), share)

        def column(t, carry):
            low = pl.ds(pl.multiple_of(t * tile, tile), tile)
            term = jnp.dot(re, cos_v[view, low], preferred_element_type=jnp.float32) - jnp.dot(
                im, sin_v[view, low], preferred_element_type=jnp.float32
            )
            if first:
                out_ref[:, low] = term * scale
            else:
                out_ref[:, low] += term * scale
            return carry

        lax.fori_loop(0, cols // tile, column, 0)

    accumulate(send_b[me, 0], send_b[me, 1], me, True)

    def back_step(k, carry):
        for part in range(parts):
            inward(k, part).wait()
        accumulate(recv_b[k, 0], recv_b[k, 1], lax.rem(me + n - k, n), False)
        return carry

    lax.fori_loop(1, n, back_step, 0)


def convolve_kernel(n, normed, spectrum):
    rows, cols = normed.shape
    share = cols // n
    index = np.arange(cols)
    angle = (index[:, None] * index[None, :] % cols) * (2.0 * math.pi / cols)
    cos_m = jnp.asarray(np.cos(angle).astype(jnp.bfloat16))
    sin_m = jnp.asarray(np.sin(angle).astype(jnp.bfloat16))
    pos = lax.axis_index("seq")
    turn = 2.0 * math.pi / (n * cols)
    twist = (jnp.arange(cols, dtype=jnp.int32) * pos).astype(jnp.float32)[None] * turn
    owned = pos * share + jnp.arange(share, dtype=jnp.int32)
    undo = (jnp.arange(n, dtype=jnp.int32)[:, None] * owned[None]).astype(jnp.float32) * turn
    parts = 4 if rows % 64 == 0 else 1
    block = pltpu.VMEM((n, 2, rows, share), jnp.bfloat16)
    dma = pltpu.SemaphoreType.DMA
    return pl.pallas_call(
        functools.partial(conv_kernel, n),
        out_shape=jax.ShapeDtypeStruct((rows, cols), jnp.float32),
        in_specs=[vmem_spec()] + [pl.BlockSpec(memory_space=pl.ANY)] * 3 + [vmem_spec()] * 4,
        out_specs=vmem_spec(),
        scratch_shapes=[
            pltpu.VMEM((cols, cols), jnp.bfloat16),
            pltpu.VMEM((cols, cols), jnp.bfloat16),
            pltpu.VMEM(spectrum.shape, jnp.float32),
            block, block, block, block,
            dma((n, 2)), dma((1,)), dma((n,)), dma((n,)), dma((n, parts)), dma((n, parts)),
        ],
        compiler_params=pltpu.CompilerParams(
            collective_id=1, has_side_effects=True, vmem_limit_bytes=VMEM_BYTES
        ),
    )(normed, spectrum, cos_m, sin_m, jnp.cos(twist), jnp.sin(twist), jnp.cos(undo), jnp.sin(undo))


def across(left, right):
    return lax.dot_general(
        left, right, (((0,), (0,)), ((), ())), preferred_element_type=jnp.float32
    )


def mlp_kernel(
    n, width, tok_ref, conv_ref, norm_ref, skip_ref, gain_ref, mi_ref, up_ref, down_ref, mo_ref,
    out_ref, resid, stats, first, regrouped, lowered, returned,
    st_send, st_recv, send_sem, recv_sem,
):
    me = lax.axis_index("chan")
    barrier = greet("chan", n)
    rows, cols = tok_ref.shape
    chunks, _, step = first.shape
    piece = rows // n

    def residual_of(c, carry):
        view = pl.ds(pl.multiple_of(c * step, step), step)
        value = (
            tok_ref[:, view].astype(jnp.float32)
            + conv_ref[:, view]
            + skip_ref[...] * norm_ref[:, view].astype(jnp.float32)
        ).astype(jnp.bfloat16)
        resid[:, view] = value
        value = value.astype(jnp.float32)
        stats[0, 0:1, view] = jnp.sum(value, axis=0, keepdims=True)
        stats[0, 1:2, view] = jnp.sum(value * value, axis=0, keepdims=True)
        return carry

    lax.fori_loop(0, chunks, residual_of, 0)
    total = share_stats(n, barrier, stats, st_send, st_recv)
    mean = total[0:1] / width
    stats[0, 0:1, :] = mean
    stats[0, 1:2, :] = lax.rsqrt(total[1:2] / width - mean * mean + 1e-05)

    def exchange(phase, c, k):
        peer = lax.rem(me + k, n)
        source, target = ((first, regrouped), (lowered, returned))[phase]
        return pltpu.make_async_remote_copy(
            src_ref=source.at[c, pl.ds(pl.multiple_of(peer * piece, 16), piece)],
            dst_ref=target.at[c, pl.ds(pl.multiple_of(me * piece, 16), piece)],
            send_sem=send_sem.at[phase, c, k],
            recv_sem=recv_sem.at[phase, c, k],
            device_id={"chan": peer},
            device_id_type=MESH,
        )

    own = pl.ds(pl.multiple_of(me * piece, 16), piece)

    def first_step(c, carry):
        view = pl.ds(pl.multiple_of(c * step, step), step)
        value = resid[:, view].astype(jnp.float32)
        value = (value - stats[0, 0:1, view]) * stats[0, 1:2, view] * gain_ref[...]
        first[c] = across(mi_ref[...], value.astype(jnp.bfloat16)).astype(jnp.bfloat16)
        for k in range(1, n):
            exchange(0, c, k).start()
        regrouped[c, own] = first[c, own]
        return carry

    lax.fori_loop(0, chunks, first_step, 0)

    def second_step(c, carry):
        for k in range(1, n):
            exchange(0, c, k).wait()
        pre = across(up_ref[...], regrouped[c])
        hidden = 0.5 * pre * (1.0 + lax.erf(pre * math.sqrt(0.5)))
        lowered[c] = across(down_ref[...], hidden.astype(jnp.bfloat16)).astype(jnp.bfloat16)
        for k in range(1, n):
            exchange(1, c, k).start()
        returned[c, own] = lowered[c, own]
        return carry

    lax.fori_loop(0, chunks, second_step, 0)

    def third_step(c, carry):
        view = pl.ds(pl.multiple_of(c * step, step), step)
        for k in range(1, n):
            exchange(1, c, k).wait()
        term = across(mo_ref[...], returned[c])
        out_ref[:, view] = (resid[:, view].astype(jnp.float32) + term).astype(jnp.bfloat16)
        return carry

    lax.fori_loop(0, chunks, third_step, 0)


def mlp(n, width, *operands):
    rows, cols = operands[0].shape
    step = 256 if cols % 256 == 0 else cols
    chunks = cols // step
    block = pltpu.VMEM((chunks, rows, step), jnp.bfloat16)
    dma = pltpu.SemaphoreType.DMA
    return pl.pallas_call(
        functools.partial(mlp_kernel, n, width),
        out_shape=jax.ShapeDtypeStruct((rows, cols), jnp.bfloat16),
        in_specs=[vmem_spec()] * len(operands),
        out_specs=vmem_spec(),
        scratch_shapes=[
            pltpu.VMEM((rows, cols), jnp.bfloat16),
            pltpu.VMEM((n, 2, cols), jnp.float32),
            block, block, block, block,
            dma((n,)), dma((n,)), dma((2, chunks, n)), dma((2, chunks, n)),
        ],
        compiler_params=pltpu.CompilerParams(
            collective_id=2, has_side_effects=True, vmem_limit_bytes=VMEM_BYTES
        ),
    )(*operands)


def shards(
    tokens,
    filter_spectrum,
    skip_weight,
    norm_gain,
    mlp_gain,
    mix_in,
    up_weight,
    down_weight,
    mix_out,
):
    columns, tok_rows = tokens.shape
    groups = lax.axis_size("seq")
    blocks = lax.axis_size("chan")
    width = columns * blocks
    normed = first_norm(blocks, width, tokens, norm_gain)
    if groups == 8 and (tok_rows // groups) % 128 == 0:
        convolved = convolve_kernel(groups, normed, filter_spectrum)
    else:
        cos_w, sin_w = dft_tables(RADIX)
        cos_a, sin_a = dft_tables(tok_rows // RADIX)
        cos_p, sin_p = dft_tables(groups)

        def swap(pair_in):
            return tuple(
                lax.all_to_all(half, "seq", split_axis=1, concat_axis=1, tiled=True)
                for half in pair_in
            )

        convolved = spectral(
            normed, filter_spectrum, (cos_w, sin_w, cos_a, sin_a), cos_p, sin_p, swap, swap
        )
    hidden_width = up_weight.shape[1] // columns
    return mlp(
        blocks,
        width,
        tokens,
        convolved,
        normed,
        skip_weight[:, None],
        mlp_gain[:, None],
        mix_in.reshape(columns, columns),
        up_weight.reshape(columns, hidden_width),
        down_weight.reshape(hidden_width, columns),
        mix_out.reshape(columns, columns),
    )


def solution(mesh):
    in_specs = (
        P("chan", "seq"),
        P(None, "chan", "seq"),
        P("chan"),
        P("chan"),
        P("chan"),
        P("chan", None),
        P("chan", None),
        P("chan", None),
        P("chan", None),
    )
    out_specs = P("chan", "seq")
    return jax.shard_map(shards, mesh=mesh, in_specs=in_specs, out_specs=out_specs, check_vma=False)
```

profile of v0, /device:TPU:0, one launch (start us, length us, event | category | flops | bytes accessed | tf_op | source)
XLA Modules:
  0.0 133.0 jit_solution(6808221604900056223)
XLA Ops:
  0.0 0.7 fusion
  0.7 0.9 fusion.2
  1.5 1.3 reduce
  2.8 0.7 reshape.39.mi_ref
  3.6 1.3 reduce.3
  4.9 0.7 reshape.42.mo_ref
  5.6 1.4 %copy.13.skip_ref = f32[192,1]{1,0:T(8,128)} copy(f32[192,1]{0,1:T(1,128)} %bitcast.3) | data formatting | bytes 1536 | tf_op jit(solution)/shard_map/broadcast_in_dim | solution.py:541
  7.1 1.4 %copy.12.gain_ref = f32[192,1]{1,0:T(8,128)} copy(f32[192,1]{0,1:T(1,128)} %bitcast.4) | data formatting | bytes 1536 | tf_op jit(solution)/shard_map/broadcast_in_dim | solution.py:184
  8.5 1.4 %copy.14.gain_ref = f32[192,1]{1,0:T(8,128)} copy(f32[192,1]{0,1:T(1,128)} %bitcast.5) | data formatting | bytes 1536 | tf_op jit(solution)/shard_map/broadcast_in_dim | solution.py:542
  9.9 7.1 %reduce.1 = bf16[147456]{0:T(1024)(128)(2,1)S(1)} reduce(bf16[1,147456]{1,0:T(2,128)(2,1)} %param.17, bf16[]{:T(256)} %constant.21), dimensions={0}, to_apply=%param.17.reduce_sub_computation | reduce | bytes 589826 | tf_op args[6]
  17.0 1.0 reshape.40.up_ref
  18.0 7.1 %reduce.2 = bf16[147456]{0:T(1024)(128)(2,1)S(1)} reduce(bf16[1,147456]{1,0:T(2,128)(2,1)} %param.18, bf16[]{:T(256)} %constant.21), dimensions={0}, to_apply=%param.18.reduce_sub_computation | reduce | bytes 589826 | tf_op args[7]
  25.1 1.0 reshape.41.down_ref
  26.1 9.9 %shard_map.109.x_ref.norm_ref = bf16[192,2048]{1,0:T(8,128)(2,1)} custom-call(bf16[192,2048]{1,0:T(8,128)(2,1)} %tok_ref.1, f32[192,1]{1,0:T(8,128)} %copy.12.gain_ref), custom_call_target="tpu_custom_call" | custom-call | tf_op jit(solution)/shard_map/pallas_call | solution.py:171
  36.0 49.6 %shard_map.110.conv_ref = f32[192,2048]{1,0:T(8,128)} custom-call(bf16[192,2048]{1,0:T(8,128)(2,1)} %shard_map.109.x_ref.norm_ref, f32[2,192,2048]{2,1,0:T(8,128)} %filt_hbm.1, bf16[2048,2048]{1,0:T(8,128)(2,1)} %constant.15.clone.cos_hbm, bf16[2048,2048]{1,0:T(8,128)(2,1)} %constant.16.clone.sin_hbm, f32[1,2048]{1,0:T(1,128)} %get-tuple-element.8.twc_ref, ...), custom_call_target="tpu_custom_call" | custom-call | tf_op jit(solution)/shard_map/pallas_call | solution.py:375
  85.6 45.3 %shard_map.111 = bf16[192,2048]{1,0:T(8,128)(2,1)} custom-call(bf16[192,2048]{1,0:T(8,128)(2,1)} %tok_ref.1, f32[192,2048]{1,0:T(8,128)} %shard_map.110.conv_ref, bf16[192,2048]{1,0:T(8,128)(2,1)} %shard_map.109.x_ref.norm_ref, f32[192,1]{1,0:T(8,128)} %copy.13.skip_ref, f32[192,1]{1,0:T(8,128)} %copy.14.gain_ref, bf16[192,192]{1,0:T(8,128)(2,1)} %reshape.39.mi_ref, ...), custom_call_target="tpu_custom_call" | custom-call | tf_op jit(solution)/shard_map/pallas_call | solution.py:485
  130.9 2.1 %copy.16 = bf16[192,2048]{1,0:T(8,128)(2,1)} copy(bf16[192,2048]{1,0:T(8,128)(2,1)} %shard_map.111) | data formatting | bytes 1572864
  (1 shorter events, 0.0 us)
where the time goes:
time: 133 us
  Pallas kernels  105 us (79%)
  other arithmetic  18.3 us (14%)
  local copies, waits for them, and re-layouts  9.9 us (7%)
    pallas_call x1, Pallas kernels, convolve_kernel(): pl.pallas_call(functools.partial(conv_kernel, n), out_shape=jax.ShapeDtyp...  49.6 us
    pallas_call x1, Pallas kernels, mlp(): pl.pallas_call(functools.partial(mlp_kernel, n, width), out_shape=jax.Sha...  45.3 us
    unnamed x4, other arithmetic  16.8 us
    pallas_call x1, Pallas kernels, first_norm(): pl.pallas_call(functools.partial(norm_kernel, n, width), out_shape=jax.Sh...  9.91 us

commit v1 on v0

--- a/solution.py
+++ b/solution.py
@@ -116,6 +116,30 @@
     return pl.BlockSpec(memory_space=pltpu.VMEM)
 
 
+def column_of(row_ref):
+    size = row_ref.shape[1]
+    shape = (size, size)
+    on = lax.broadcasted_iota(jnp.int32, shape, 0) == lax.broadcasted_iota(jnp.int32, shape, 1)
+    return jnp.sum(jnp.where(on, row_ref[...], 0.0), axis=1, keepdims=True)
+
+
+def unfold(flat_ref, wide, out_ref):
+    rows, cols = out_ref.shape
+    pack = 1 if cols % 128 == 0 else 2
+    batch = 8 // pack
+
+    def step(i, carry):
+        low = pl.multiple_of(i * (8 * cols), 128)
+        for j in range(batch):
+            run = flat_ref[0:1, pl.ds(low + j * pack * cols, pack * cols)].astype(jnp.float32)
+            for m in range(pack):
+                wide[pl.ds(i * 8 + j * pack + m, 1), 0:cols] = run[:, m * cols : (m + 1) * cols]
+        return carry
+
+    lax.fori_loop(0, rows // 8, step, 0)
+    out_ref[...] = wide[0:rows, 0:cols].astype(jnp.bfloat16)
+
+
 def greet(axis, n):
     me = lax.axis_index(axis)
     barrier = pltpu.get_barrier_semaphore()
@@ -160,7 +184,7 @@
     total = share_stats(n, barrier, stats, send_sem, recv_sem)
     mean = total[0:1] / width
     scale = lax.rsqrt(total[1:2] / width - mean * mean + 1e-05)
-    gain = gain_ref[...]
+    gain = column_of(gain_ref)
     for c in range(0, cols, step):
         x = x_ref[:, c : c + step].astype(jnp.float32)
         y = (x - mean[:, c : c + step]) * scale[:, c : c + step] * gain
@@ -181,7 +205,7 @@
         compiler_params=pltpu.CompilerParams(
             collective_id=0, has_side_effects=True, vmem_limit_bytes=VMEM_BYTES
         ),
-    )(tokens, gain[:, None])
+    )(tokens, gain[None])
 
 
 def small_dft(values, sign):
@@ -208,7 +232,8 @@
 
 
 def conv_kernel(
-    n, x_ref, filt_hbm, cos_hbm, sin_hbm, twc_ref, tws_ref, undo_c, undo_s, out_ref,
+    n, x_ref, filt_hbm, cos_hbm, sin_hbm, twc_ref, tws_ref, undo_c, undo_s,
+    mi_flat, up_flat, down_flat, mo_flat, out_ref, mi_ref, up_ref, down_ref, mo_ref, wide,
     cos_v, sin_v, filt_v, send_f, recv_f, send_b, recv_b,
     load_sem, filt_sem, sf_sem, rf_sem, sb_sem, rb_sem,
 ):
@@ -269,6 +294,10 @@
     re, im = transform(0)
     recv_f[me, 0] = re
     recv_f[me, 1] = im
+    for flat, square in (
+        (mi_flat, mi_ref), (up_flat, up_ref), (down_flat, down_ref), (mo_flat, mo_ref)
+    ):
+        unfold(flat, wide, square)
     filt_copy.wait()
 
     def arrive(k, carry):
@@ -357,8 +386,10 @@
     lax.fori_loop(1, n, back_step, 0)
 
 
-def convolve_kernel(n, normed, spectrum):
+def convolve_kernel(n, normed, spectrum, flats):
     rows, cols = normed.shape
+    hidden = flats[1].shape[1] // rows
+    shapes = [(rows, rows), (rows, hidden), (hidden, rows), (rows, rows)]
     share = cols // n
     index = np.arange(cols)
     angle = (index[:, None] * index[None, :] % cols) * (2.0 * math.pi / cols)
@@ -374,10 +405,12 @@
     dma = pltpu.SemaphoreType.DMA
     return pl.pallas_call(
         functools.partial(conv_kernel, n),
-        out_shape=jax.ShapeDtypeStruct((rows, cols), jnp.float32),
-        in_specs=[vmem_spec()] + [pl.BlockSpec(memory_space=pl.ANY)] * 3 + [vmem_spec()] * 4,
-        out_specs=vmem_spec(),
+        out_shape=[jax.ShapeDtypeStruct((rows, cols), jnp.float32)]
+        + [jax.ShapeDtypeStruct(shape, jnp.bfloat16) for shape in shapes],
+        in_specs=[vmem_spec()] + [pl.BlockSpec(memory_space=pl.ANY)] * 3 + [vmem_spec()] * 8,
+        out_specs=[vmem_spec()] * 5,
         scratch_shapes=[
+            pltpu.VMEM((max(rows, hidden),) * 2, jnp.float32),
             pltpu.VMEM((cols, cols), jnp.bfloat16),
             pltpu.VMEM((cols, cols), jnp.bfloat16),
             pltpu.VMEM(spectrum.shape, jnp.float32),
@@ -387,7 +420,7 @@
         compiler_params=pltpu.CompilerParams(
             collective_id=1, has_side_effects=True, vmem_limit_bytes=VMEM_BYTES
         ),
-    )(normed, spectrum, cos_m, sin_m, jnp.cos(twist), jnp.sin(twist), jnp.cos(undo), jnp.sin(undo))
+    )(normed, spectrum, cos_m, sin_m, jnp.cos(twist), jnp.sin(twist), jnp.cos(undo), jnp.sin(undo), *flats)
 
 
 def across(left, right):
@@ -406,13 +439,14 @@
     rows, cols = tok_ref.shape
     chunks, _, step = first.shape
     piece = rows // n
+    skip, gain = column_of(skip_ref), column_of(gain_ref)
 
     def residual_of(c, carry):
         view = pl.ds(pl.multiple_of(c * step, step), step)
         value = (
             tok_ref[:, view].astype(jnp.float32)
             + conv_ref[:, view]
-            + skip_ref[...] * norm_ref[:, view].astype(jnp.float32)
+            + skip * norm_ref[:, view].astype(jnp.float32)
         ).astype(jnp.bfloat16)
         resid[:, view] = value
         value = value.astype(jnp.float32)
@@ -443,7 +477,7 @@
     def first_step(c, carry):
         view = pl.ds(pl.multiple_of(c * step, step), step)
         value = resid[:, view].astype(jnp.float32)
-        value = (value - stats[0, 0:1, view]) * stats[0, 1:2, view] * gain_ref[...]
+        value = (value - stats[0, 0:1, view]) * stats[0, 1:2, view] * gain
         first[c] = across(mi_ref[...], value.astype(jnp.bfloat16)).astype(jnp.bfloat16)
         for k in range(1, n):
             exchange(0, c, k).start()
@@ -515,8 +549,10 @@
     blocks = lax.axis_size("chan")
     width = columns * blocks
     normed = first_norm(blocks, width, tokens, norm_gain)
+    hidden_width = up_weight.shape[1] // columns
+    flats = (mix_in, up_weight, down_weight, mix_out)
     if groups == 8 and (tok_rows // groups) % 128 == 0:
-        convolved = convolve_kernel(groups, normed, filter_spectrum)
+        convolved, *factors = convolve_kernel(groups, normed, filter_spectrum, flats)
     else:
         cos_w, sin_w = dft_tables(RADIX)
         cos_a, sin_a = dft_tables(tok_rows // RADIX)
@@ -531,19 +567,17 @@
         convolved = spectral(
             normed, filter_spectrum, (cos_w, sin_w, cos_a, sin_a), cos_p, sin_p, swap, swap
         )
-    hidden_width = up_weight.shape[1] // columns
+        shapes = ((columns, columns), (columns, hidden_width), (hidden_width, columns))
+        factors = [flat.reshape(shape) for flat, shape in zip(flats, shapes + shapes[:1])]
     return mlp(
         blocks,
         width,
         tokens,
         convolved,
         normed,
-        skip_weight[:, None],
-        mlp_gain[:, None],
-        mix_in.reshape(columns, columns),
-        up_weight.reshape(columns, hidden_width),
-        down_weight.reshape(hidden_width, columns),
-        mix_out.reshape(columns, columns),
+        skip_weight[None],
+        mlp_gain[None],
+        *factors,
     )
 
 

time: 133 us -> 109 us (0.82)
  other arithmetic: 18.3 us -> 1.51 us
  local copies, waits for them, and re-layouts: 9.9 us -> 2.09 us
    unnamed x4 -> x0, other arithmetic: 16.8 us -> none
    broadcast_in_dim x3 -> x0, local copies, waits for them, and re-layouts: 4.31 us -> none  [the longest x1 1.45 us: shards(): skip_weight[:, None]]
    reshape x4 -> x0, local copies, waits for them, and re-layouts: 3.5 us -> none  [the longest x1 1.03 us: shards(): down_weight.reshape(hidden_width, columns)]
where the time goes in v1:
time: 109 us
  Pallas kernels  105 us (96%)
  local copies, waits for them, and re-layouts  2.09 us (2%)
  other arithmetic  1.51 us (1%)
    pallas_call x1, Pallas kernels, convolve_kernel(): pl.pallas_call(functools.partial(conv_kernel, n), out_shape=[jax.ShapeDty...  50.3 us
    pallas_call x1, Pallas kernels, mlp(): pl.pallas_call(functools.partial(mlp_kernel, n, width), out_shape=jax.Sha...  45.2 us
    pallas_call x1, Pallas kernels, first_norm(): pl.pallas_call(functools.partial(norm_kernel, n, width), out_shape=jax.Sh...  9.92 us

profile of v1, /device:TPU:0, one launch (start us, length us, event | category | flops | bytes accessed | tf_op | source)
XLA Modules:
  0.0 109.1 jit_solution(2084905037278322120)
XLA Ops:
  0.0 0.7 fusion
  0.7 0.9 fusion.2
  1.5 9.9 %shard_map.109.x_ref.norm_ref = bf16[192,2048]{1,0:T(8,128)(2,1)} custom-call(bf16[192,2048]{1,0:T(8,128)(2,1)} %tok_ref.1, f32[1,192]{1,0:T(1,128)} %bitcast.5), custom_call_target="tpu_custom_call" | custom-call | tf_op jit(solution)/shard_map/pallas_call | solution.py:195
  11.4 50.3 %shard_map.110 = (f32[192,2048]{1,0:T(8,128)}, bf16[192,192]{1,0:T(8,128)(2,1)}, bf16[192,768]{1,0:T(8,128)(2,1)}, bf16[768,192]{1,0:T(8,128)(2,1)}, bf16[192,192]{1,0:T(8,128)(2,1)}) custom-call(bf16[192,2048]{1,0:T(8,128)(2,1)} %shard_map.109.x_ref.norm_ref, f32[2,192,2048]{2,1,0:T(8,128)} %filt_hbm.1, bf16[2048,2048]{1,0:T(8,128)(2,1)} %constant.15.clone.cos_hbm, ...), custom_call_target="tpu_custom_call" | custom-call | tf_op jit(solution)/shard_map/pallas_call | solution.py:406
  61.8 45.2 %shard_map.111 = bf16[192,2048]{1,0:T(8,128)(2,1)} custom-call(bf16[192,2048]{1,0:T(8,128)(2,1)} %tok_ref.1, f32[192,2048]{1,0:T(8,128)} %get-tuple-element.10.conv_ref, bf16[192,2048]{1,0:T(8,128)(2,1)} %shard_map.109.x_ref.norm_ref, f32[1,192]{1,0:T(1,128)} %bitcast.3, f32[1,192]{1,0:T(1,128)} %bitcast.4, bf16[192,192]{1,0:T(8,128)(2,1)} %get-tuple-element.11.mi_ref, ...), custom_call_target="tpu_custom_call" | custom-call | tf_op jit(solution)/shard_map/pallas_call | solution.py:519
  107.0 2.1 %copy.13 = bf16[192,2048]{1,0:T(8,128)(2,1)} copy(bf16[192,2048]{1,0:T(8,128)(2,1)} %shard_map.111) | data formatting | bytes 1572864
  (1 shorter events, 0.0 us)

commit v2 on v1

--- a/solution.py
+++ b/solution.py
@@ -150,9 +150,8 @@
     return barrier
 
 
-def share_stats(n, barrier, stats, send_sem, recv_sem):
+def share_stats(n, stats, send_sem, recv_sem):
     me = lax.axis_index("chan")
-    pl.semaphore_wait(barrier, n - 1)
     copies = []
     for k in range(1, n):
         copy = pltpu.make_async_remote_copy(
@@ -175,13 +174,18 @@
 
 def norm_kernel(n, width, x_ref, gain_ref, out_ref, stats, send_sem, recv_sem):
     barrier = greet("chan", n)
+    norm_body(n, width, barrier, n - 1, x_ref, gain_ref, out_ref, stats, send_sem, recv_sem)
+
+
+def norm_body(n, width, barrier, signals, x_ref, gain_ref, out_ref, stats, send_sem, recv_sem):
     cols = x_ref.shape[1]
     step = min(cols, 512)
     for c in range(0, cols, step):
         x = x_ref[:, c : c + step].astype(jnp.float32)
         stats[0, 0:1, c : c + step] = jnp.sum(x, axis=0, keepdims=True)
         stats[0, 1:2, c : c + step] = jnp.sum(x * x, axis=0, keepdims=True)
-    total = share_stats(n, barrier, stats, send_sem, recv_sem)
+    pl.semaphore_wait(barrier, signals)
+    total = share_stats(n, stats, send_sem, recv_sem)
     mean = total[0:1] / width
     scale = lax.rsqrt(total[1:2] / width - mean * mean + 1e-05)
     gain = column_of(gain_ref)
@@ -232,13 +236,16 @@
 
 
 def conv_kernel(
-    n, x_ref, filt_hbm, cos_hbm, sin_hbm, twc_ref, tws_ref, undo_c, undo_s,
-    mi_flat, up_flat, down_flat, mo_flat, out_ref, mi_ref, up_ref, down_ref, mo_ref, wide,
-    cos_v, sin_v, filt_v, send_f, recv_f, send_b, recv_b,
-    load_sem, filt_sem, sf_sem, rf_sem, sb_sem, rb_sem,
+    n, n_chan, width, tok_ref, gain_ref, filt_hbm, cos_hbm, sin_hbm,
+    twc_ref, tws_ref, undo_c, undo_s,
+    mi_flat, up_flat, down_flat, mo_flat,
+    out_ref, x_ref, mi_ref, up_ref, down_ref, mo_ref, wide,
+    cos_v, sin_v, filt_v, send_f, recv_f, send_b, recv_b, stats,
+    st_send, st_recv, load_sem, filt_sem, sf_sem, rf_sem, sb_sem, rb_sem,
 ):
     me = lax.axis_index("seq")
     barrier = greet("seq", n)
+    greet("chan", n_chan)
     rows, cols = x_ref.shape
     share = cols // n
     parts = sb_sem.shape[1]
@@ -257,61 +264,57 @@
         load(k, 0).start()
         load(k, 1).start()
     filt_copy.start()
-    pl.semaphore_wait(barrier, n - 1)
-
-    def transform(k):
-        load(k, 0).wait()
-        load(k, 1).wait()
+    norm_body(
+        n_chan, width, barrier, n + n_chan - 2, tok_ref, gain_ref, x_ref, stats, st_send, st_recv
+    )
+
+    def transform(k, part):
+        if part == 0:
+            load(k, 0).wait()
+            load(k, 1).wait()
         view = block_of(k)
-        x = x_ref[...]
+        x = x_ref[part * group : (part + 1) * group, :]
         re = jnp.dot(x, cos_v[:, view], preferred_element_type=jnp.float32)
         im = -jnp.dot(x, sin_v[:, view], preferred_element_type=jnp.float32)
-        tc, ts = twc_ref[:, view], tws_ref[:, view]
+        tc, ts = twc_ref[me, :, view], tws_ref[me, :, view]
         return (
             (re * tc + im * ts).astype(jnp.bfloat16),
             (im * tc - re * ts).astype(jnp.bfloat16),
         )
 
-    def outward(k):
+    def rows_of(part):
+        return pl.ds(part * group, group)
+
+    def outward(k, part):
+        return pltpu.make_async_remote_copy(
+            src_ref=send_f.at[k, :, rows_of(part)],
+            dst_ref=recv_f.at[me, :, rows_of(part)],
+            send_sem=sf_sem.at[k, part],
+            recv_sem=rf_sem.at[k, part],
+            device_id={"seq": lax.rem(me + k, n)},
+            device_id_type=MESH,
+        )
+
+    for part in range(parts):
+
+        def forward(k, carry, part=part):
+            re, im = transform(k, part)
+            send_f[k, 0, rows_of(part)] = re
+            send_f[k, 1, rows_of(part)] = im
+            outward(k, part).start()
+            return carry
+
+        lax.fori_loop(1, n, forward, 0)
+        re, im = transform(0, part)
+        recv_f[me, 0, rows_of(part)] = re
+        recv_f[me, 1, rows_of(part)] = im
+    filt_copy.wait()
+
+    def inward(k, part):
         peer = lax.rem(me + k, n)
         return pltpu.make_async_remote_copy(
-            src_ref=send_f.at[k],
-            dst_ref=recv_f.at[me],
-            send_sem=sf_sem.at[k],
-            recv_sem=rf_sem.at[k],
-            device_id={"seq": peer},
-            device_id_type=MESH,
-        )
-
-    def forward(k, carry):
-        re, im = transform(k)
-        send_f[k, 0] = re
-        send_f[k, 1] = im
-        outward(k).start()
-        return carry
-
-    lax.fori_loop(1, n, forward, 0)
-    re, im = transform(0)
-    recv_f[me, 0] = re
-    recv_f[me, 1] = im
-    for flat, square in (
-        (mi_flat, mi_ref), (up_flat, up_ref), (down_flat, down_ref), (mo_flat, mo_ref)
-    ):
-        unfold(flat, wide, square)
-    filt_copy.wait()
-
-    def arrive(k, carry):
-        outward(k).wait()
-        return carry
-
-    lax.fori_loop(1, n, arrive, 0)
-
-    def inward(k, part):
-        peer = lax.rem(me + k, n)
-        view = pl.ds(part * group, group)
-        return pltpu.make_async_remote_copy(
-            src_ref=send_b.at[peer, :, view],
-            dst_ref=recv_b.at[k, :, view],
+            src_ref=send_b.at[peer, :, rows_of(part)],
+            dst_ref=recv_b.at[k, :, rows_of(part)],
             send_sem=sb_sem.at[k, part],
             recv_sem=rb_sem.at[k, part],
             device_id={"seq": peer},
@@ -320,6 +323,12 @@
 
     lanes = 128
     for part in range(parts):
+
+        def arrive(k, carry, part=part):
+            outward(k, part).wait()
+            return carry
+
+        lax.fori_loop(1, n, arrive, 0)
 
         def middle(i, carry, part=part):
             view = pl.ds(pl.multiple_of(part * group + i * 16, 16), 16)
@@ -342,8 +351,8 @@
                 back = small_dft(filtered, 1)
                 for p in range(n):
                     br, bi = back[p]
-                    uc = undo_c[p : p + 1, c : c + lanes]
-                    us = undo_s[p : p + 1, c : c + lanes]
+                    uc = undo_c[me, p : p + 1, c : c + lanes]
+                    us = undo_s[me, p : p + 1, c : c + lanes]
                     send_b[p, 0, view, c : c + lanes] = (br * uc - bi * us).astype(jnp.bfloat16)
                     send_b[p, 1, view, c : c + lanes] = (bi * uc + br * us).astype(jnp.bfloat16)
             return carry
@@ -356,10 +365,15 @@
 
         lax.fori_loop(1, n, push, 0)
 
+    for flat, square in (
+        (mi_flat, mi_ref), (up_flat, up_ref), (down_flat, down_ref), (mo_flat, mo_ref)
+    ):
+        unfold(flat, wide, square)
+
     tile = min(cols, 512)
     scale = 1.0 / (n * cols)
 
-    def accumulate(re, im, source, first):
+    def accumulate(re, im, source, part, first):
         view = pl.ds(pl.multiple_of(source * share, share), share)
 
         def column(t, carry):
@@ -368,59 +382,70 @@
                 im, sin_v[view, low], preferred_element_type=jnp.float32
             )
             if first:
-                out_ref[:, low] = term * scale
+                out_ref[rows_of(part), low] = term * scale
             else:
-                out_ref[:, low] += term * scale
+                out_ref[rows_of(part), low] += term * scale
             return carry
 
         lax.fori_loop(0, cols // tile, column, 0)
 
-    accumulate(send_b[me, 0], send_b[me, 1], me, True)
-
-    def back_step(k, carry):
-        for part in range(parts):
+    for part in range(parts):
+        accumulate(send_b[me, 0, rows_of(part)], send_b[me, 1, rows_of(part)], me, part, True)
+    for part in range(parts):
+
+        def back_step(k, carry, part=part):
             inward(k, part).wait()
-        accumulate(recv_b[k, 0], recv_b[k, 1], lax.rem(me + n - k, n), False)
-        return carry
-
-    lax.fori_loop(1, n, back_step, 0)
-
-
-def convolve_kernel(n, normed, spectrum, flats):
-    rows, cols = normed.shape
+            source = lax.rem(me + n - k, n)
+            accumulate(
+                recv_b[k, 0, rows_of(part)], recv_b[k, 1, rows_of(part)], source, part, False
+            )
+            return carry
+
+        lax.fori_loop(1, n, back_step, 0)
+
+
+def convolve_kernel(n, n_chan, width, tokens, gain, spectrum, flats):
+    rows, cols = tokens.shape
     hidden = flats[1].shape[1] // rows
-    shapes = [(rows, rows), (rows, hidden), (hidden, rows), (rows, rows)]
+    shapes = [(rows, cols), (rows, rows), (rows, hidden), (hidden, rows), (rows, rows)]
     share = cols // n
     index = np.arange(cols)
     angle = (index[:, None] * index[None, :] % cols) * (2.0 * math.pi / cols)
     cos_m = jnp.asarray(np.cos(angle).astype(jnp.bfloat16))
     sin_m = jnp.asarray(np.sin(angle).astype(jnp.bfloat16))
-    pos = lax.axis_index("seq")
     turn = 2.0 * math.pi / (n * cols)
-    twist = (jnp.arange(cols, dtype=jnp.int32) * pos).astype(jnp.float32)[None] * turn
-    owned = pos * share + jnp.arange(share, dtype=jnp.int32)
-    undo = (jnp.arange(n, dtype=jnp.int32)[:, None] * owned[None]).astype(jnp.float32) * turn
-    parts = 4 if rows % 64 == 0 else 1
+    ranks = np.arange(n)
+    twist = ranks[:, None, None] * index[None, None, :] * turn
+    owned = ranks[:, None] * share + np.arange(share)[None]
+    undo = ranks[None, :, None] * owned[:, None, :] * turn
+    small = [
+        jnp.asarray(form(angles).astype(np.float32))
+        for angles in (twist, undo)
+        for form in (np.cos, np.sin)
+    ]
+    parts = 2 if rows % 32 == 0 else 1
     block = pltpu.VMEM((n, 2, rows, share), jnp.bfloat16)
     dma = pltpu.SemaphoreType.DMA
+    pair = dma((n, parts))
     return pl.pallas_call(
-        functools.partial(conv_kernel, n),
+        functools.partial(conv_kernel, n, n_chan, width),
         out_shape=[jax.ShapeDtypeStruct((rows, cols), jnp.float32)]
         + [jax.ShapeDtypeStruct(shape, jnp.bfloat16) for shape in shapes],
-        in_specs=[vmem_spec()] + [pl.BlockSpec(memory_space=pl.ANY)] * 3 + [vmem_spec()] * 8,
-        out_specs=[vmem_spec()] * 5,
+        in_specs=[vmem_spec()] * 2 + [pl.BlockSpec(memory_space=pl.ANY)] * 3 + [vmem_spec()] * 8,
+        out_specs=[vmem_spec()] * 6,
         scratch_shapes=[
             pltpu.VMEM((max(rows, hidden),) * 2, jnp.float32),
             pltpu.VMEM((cols, cols), jnp.bfloat16),
             pltpu.VMEM((cols, cols), jnp.bfloat16),
             pltpu.VMEM(spectrum.shape, jnp.float32),
             block, block, block, block,
-            dma((n, 2)), dma((1,)), dma((n,)), dma((n,)), dma((n, parts)), dma((n, parts)),
+            pltpu.VMEM((n_chan, 2, cols), jnp.float32),
+            dma((n_chan,)), dma((n_chan,)), dma((n, 2)), dma((1,)), pair, pair, pair, pair,
         ],
         compiler_params=pltpu.CompilerParams(
             collective_id=1, has_side_effects=True, vmem_limit_bytes=VMEM_BYTES
         ),
-    )(normed, spectrum, cos_m, sin_m, jnp.cos(twist), jnp.sin(twist), jnp.cos(undo), jnp.sin(undo), *flats)
+    )(tokens, gain[None], spectrum, cos_m, sin_m, *small, *flats)
 
 
 def across(left, right):
@@ -455,7 +480,8 @@
         return carry
 
     lax.fori_loop(0, chunks, residual_of, 0)
-    total = share_stats(n, barrier, stats, st_send, st_recv)
+    pl.semaphore_wait(barrier, n - 1)
+    total = share_stats(n, stats, st_send, st_recv)
     mean = total[0:1] / width
     stats[0, 0:1, :] = mean
     stats[0, 1:2, :] = lax.rsqrt(total[1:2] / width - mean * mean + 1e-05)
@@ -548,12 +574,14 @@
     groups = lax.axis_size("seq")
     blocks = lax.axis_size("chan")
     width = columns * blocks
-    normed = first_norm(blocks, width, tokens, norm_gain)
     hidden_width = up_weight.shape[1] // columns
     flats = (mix_in, up_weight, down_weight, mix_out)
     if groups == 8 and (tok_rows // groups) % 128 == 0:
-        convolved, *factors = convolve_kernel(groups, normed, filter_spectrum, flats)
+        convolved, normed, *factors = convolve_kernel(
+            groups, blocks, width, tokens, norm_gain, filter_spectrum, flats
+        )
     else:
+        normed = first_norm(blocks, width, tokens, norm_gain)
         cos_w, sin_w = dft_tables(RADIX)
         cos_a, sin_a = dft_tables(tok_rows // RADIX)
         cos_p, sin_p = dft_tables(groups)

time: 109 us -> 110 us (level)
  Pallas kernels: 105 us -> 108 us
  other arithmetic: 1.51 us -> 0 us
    pallas_call x1, Pallas kernels: 45.2 us -> 47 us  [mlp(): pl.pallas_call(functools.partial(mlp_kernel, n, width), out_shape=jax.Sha...]
    sin x2 -> x0, other arithmetic: 1.51 us -> none  [the longest x1 0.85 us: convolve_kernel(): jnp.sin(twist)]
    pallas_call x2 -> x1, Pallas kernels: 60.2 us -> 61 us  [convolve_kernel(): pl.pallas_call(functools.partial(conv_kernel, n, n_chan, width), out_shap...]
where the time goes in v2:
time: 110 us
  Pallas kernels  108 us (98%)
  local copies, waits for them, and re-layouts  2.09 us (2%)
    pallas_call x1, Pallas kernels, convolve_kernel(): pl.pallas_call(functools.partial(conv_kernel, n, n_chan, width), out_shap...  61 us
    pallas_call x1, Pallas kernels, mlp(): pl.pallas_call(functools.partial(mlp_kernel, n, width), out_shape=jax.Sha...  47 us

profile of v2, /device:TPU:0, one launch (start us, length us, event | category | flops | bytes accessed | tf_op | source)
XLA Modules:
  0.0 110.1 jit_solution(2099711020011608736)
XLA Ops:
  0.0 61.0 %shard_map.145 = (f32[192,2048]{1,0:T(8,128)}, bf16[192,2048]{1,0:T(8,128)(2,1)}, bf16[192,192]{1,0:T(8,128)(2,1)}, bf16[192,768]{1,0:T(8,128)(2,1)}, bf16[768,1...) custom-call(bf16[192,2048]{1,0:T(8,128)(2,1)} %tok_ref.3, f32[1,192]{1,0:T(1,128)} %bitcast.3, f32[2,192,2048]{2,1,0:T(8,128)} %filt_hbm.1, ...), custom_call_target="tpu_custom_call" | custom-call | tf_op jit(solution)/shard_map/pallas_call | solution.py:430
  61.0 47.0 %shard_map.146 = bf16[192,2048]{1,0:T(8,128)(2,1)} custom-call(bf16[192,2048]{1,0:T(8,128)(2,1)} %tok_ref.3, f32[192,2048]{1,0:T(8,128)} %get-tuple-element.11.conv_ref, bf16[192,2048]{1,0:T(8,128)(2,1)} %get-tuple-element.12.norm_ref, f32[1,192]{1,0:T(1,128)} %bitcast.4, f32[1,192]{1,0:T(1,128)} %bitcast.5, bf16[192,192]{1,0:T(8,128)(2,1)} %get-tuple-element.13.mi_ref, ...), custom_call_target="tpu_custom_call" | custom-call | tf_op jit(solution)/shard_map/pallas_call | solution.py:545
  108.0 2.1 %copy.17 = bf16[192,2048]{1,0:T(8,128)(2,1)} copy(bf16[192,2048]{1,0:T(8,128)(2,1)} %shard_map.146) | data formatting | bytes 1572864

commit v3 on v2

--- a/solution.py
+++ b/solution.py
@@ -248,8 +248,10 @@
     greet("chan", n_chan)
     rows, cols = x_ref.shape
     share = cols // n
-    parts = sb_sem.shape[1]
+    parts = sf_sem.shape[1]
     group = rows // parts
+    pieces = sb_sem.shape[1]
+    piece = rows // pieces
 
     def block_of(k):
         return pl.ds(pl.multiple_of(lax.rem(me + k, n) * share, share), share)
@@ -312,9 +314,10 @@
 
     def inward(k, part):
         peer = lax.rem(me + k, n)
+        view = pl.ds(part * piece, piece)
         return pltpu.make_async_remote_copy(
-            src_ref=send_b.at[peer, :, rows_of(part)],
-            dst_ref=recv_b.at[k, :, rows_of(part)],
+            src_ref=send_b.at[peer, :, view],
+            dst_ref=recv_b.at[k, :, view],
             send_sem=sb_sem.at[k, part],
             recv_sem=rb_sem.at[k, part],
             device_id={"seq": peer},
@@ -322,6 +325,11 @@
         )
 
     lanes = 128
+    for flat, square in (
+        (mi_flat, mi_ref), (up_flat, up_ref), (down_flat, down_ref), (mo_flat, mo_ref)
+    ):
+        unfold(flat, wide, square)
+
     for part in range(parts):
 
         def arrive(k, carry, part=part):
@@ -330,8 +338,10 @@
 
         lax.fori_loop(1, n, arrive, 0)
 
+    for part in range(pieces):
+
         def middle(i, carry, part=part):
-            view = pl.ds(pl.multiple_of(part * group + i * 16, 16), 16)
+            view = pl.ds(pl.multiple_of(part * piece + i * 16, 16), 16)
             for c in range(0, share, lanes):
                 values = [
                     (
@@ -357,18 +367,13 @@
                     send_b[p, 1, view, c : c + lanes] = (bi * uc + br * us).astype(jnp.bfloat16)
             return carry
 
-        lax.fori_loop(0, group // 16, middle, 0)
+        lax.fori_loop(0, piece // 16, middle, 0)
 
         def push(k, carry, part=part):
             inward(k, part).start()
             return carry
 
         lax.fori_loop(1, n, push, 0)
-
-    for flat, square in (
-        (mi_flat, mi_ref), (up_flat, up_ref), (down_flat, down_ref), (mo_flat, mo_ref)
-    ):
-        unfold(flat, wide, square)
 
     tile = min(cols, 512)
     scale = 1.0 / (n * cols)
@@ -394,7 +399,8 @@
     for part in range(parts):
 
         def back_step(k, carry, part=part):
-            inward(k, part).wait()
+            for sub in range(pieces // parts):
+                inward(k, part * (pieces // parts) + sub).wait()
             source = lax.rem(me + n - k, n)
             accumulate(
                 recv_b[k, 0, rows_of(part)], recv_b[k, 1, rows_of(part)], source, part, False
@@ -423,10 +429,10 @@
         for angles in (twist, undo)
         for form in (np.cos, np.sin)
     ]
-    parts = 2 if rows % 32 == 0 else 1
+    pieces = 4 if rows % 64 == 0 else 1
     block = pltpu.VMEM((n, 2, rows, share), jnp.bfloat16)
     dma = pltpu.SemaphoreType.DMA
-    pair = dma((n, parts))
+    whole, cut = dma((n, 1)), dma((n, pieces))
     return pl.pallas_call(
         functools.partial(conv_kernel, n, n_chan, width),
         out_shape=[jax.ShapeDtypeStruct((rows, cols), jnp.float32)]
@@ -440,7 +446,7 @@
             pltpu.VMEM(spectrum.shape, jnp.float32),
             block, block, block, block,
             pltpu.VMEM((n_chan, 2, cols), jnp.float32),
-            dma((n_chan,)), dma((n_chan,)), dma((n, 2)), dma((1,)), pair, pair, pair, pair,
+            dma((n_chan,)), dma((n_chan,)), dma((n, 2)), dma((1,)), whole, whole, cut, cut,
         ],
         compiler_params=pltpu.CompilerParams(
             collective_id=1, has_side_effects=True, vmem_limit_bytes=VMEM_BYTES

time: 110 us -> 104 us (0.945)
  Pallas kernels: 108 us -> 102 us
    pallas_call x1, Pallas kernels: 61 us -> 57.3 us  [convolve_kernel(): pl.pallas_call(functools.partial(conv_kernel, n, n_chan, width), out_shap...]
    pallas_call x1, Pallas kernels: 47 us -> 44.7 us  [mlp(): pl.pallas_call(functools.partial(mlp_kernel, n, width), out_shape=jax.Sha...]
where the time goes in v3:
time: 104 us
  Pallas kernels  102 us (98%)
  local copies, waits for them, and re-layouts  2.09 us (2%)
    pallas_call x1, Pallas kernels, convolve_kernel(): pl.pallas_call(functools.partial(conv_kernel, n, n_chan, width), out_shap...  57.3 us
    pallas_call x1, Pallas kernels, mlp(): pl.pallas_call(functools.partial(mlp_kernel, n, width), out_shape=jax.Sha...  44.7 us
    unnamed x1, local copies, waits for them, and re-layouts  2.09 us

profile of v3, /device:TPU:0, one launch (start us, length us, event | category | flops | bytes accessed | tf_op | source)
XLA Modules:
  0.0 104.1 jit_solution(15304482461999781469)
XLA Ops:
  0.0 57.3 %shard_map.145 = (f32[192,2048]{1,0:T(8,128)}, bf16[192,2048]{1,0:T(8,128)(2,1)}, bf16[192,192]{1,0:T(8,128)(2,1)}, bf16[192,768]{1,0:T(8,128)(2,1)}, bf16[768,1...) custom-call(bf16[192,2048]{1,0:T(8,128)(2,1)} %tok_ref.3, f32[1,192]{1,0:T(1,128)} %bitcast.3, f32[2,192,2048]{2,1,0:T(8,128)} %filt_hbm.1, ...), custom_call_target="tpu_custom_call" | custom-call | tf_op jit(solution)/shard_map/pallas_call | solution.py:436
  57.3 44.7 %shard_map.146 = bf16[192,2048]{1,0:T(8,128)(2,1)} custom-call(bf16[192,2048]{1,0:T(8,128)(2,1)} %tok_ref.3, f32[192,2048]{1,0:T(8,128)} %get-tuple-element.11.conv_ref, bf16[192,2048]{1,0:T(8,128)(2,1)} %get-tuple-element.12.norm_ref, f32[1,192]{1,0:T(1,128)} %bitcast.4, f32[1,192]{1,0:T(1,128)} %bitcast.5, bf16[192,192]{1,0:T(8,128)(2,1)} %get-tuple-element.13.mi_ref, ...), custom_call_target="tpu_custom_call" | custom-call | tf_op jit(solution)/shard_map/pallas_call | solution.py:551
  102.0 2.1 %copy.17 = bf16[192,2048]{1,0:T(8,128)(2,1)} copy(bf16[192,2048]{1,0:T(8,128)(2,1)} %shard_map.146) | data formatting | bytes 1572864

commit v4 on v3

--- a/solution.py
+++ b/solution.py
@@ -544,7 +544,7 @@
 
 def mlp(n, width, *operands):
     rows, cols = operands[0].shape
-    step = 256 if cols % 256 == 0 else cols
+    step = 512 if cols % 512 == 0 else cols
     chunks = cols // step
     block = pltpu.VMEM((chunks, rows, step), jnp.bfloat16)
     dma = pltpu.SemaphoreType.DMA

time: 104 us -> 104 us (level)
  no operation moved by 1% of the time
where the time goes in v4:
time: 104 us; the launch traced here: 103 us
  Pallas kernels  101 us (97%)
  local copies, waits for them, and re-layouts  2.09 us (2%)
    pallas_call x1, Pallas kernels, convolve_kernel(): pl.pallas_call(functools.partial(conv_kernel, n, n_chan, width), out_shap...  57.3 us
    pallas_call x1, Pallas kernels, mlp(): pl.pallas_call(functools.partial(mlp_kernel, n, width), out_shape=jax.Sha...  43.9 us
    unnamed x1, local copies, waits for them, and re-layouts  2.09 us

profile of v4, /device:TPU:0, one launch (start us, length us, event | category | flops | bytes accessed | tf_op | source)
XLA Modules:
  0.0 103.3 jit_solution(13945618032082808371)
XLA Ops:
  0.0 57.3 %shard_map.145 = (f32[192,2048]{1,0:T(8,128)}, bf16[192,2048]{1,0:T(8,128)(2,1)}, bf16[192,192]{1,0:T(8,128)(2,1)}, bf16[192,768]{1,0:T(8,128)(2,1)}, bf16[768,1...) custom-call(bf16[192,2048]{1,0:T(8,128)(2,1)} %tok_ref.3, f32[1,192]{1,0:T(1,128)} %bitcast.3, f32[2,192,2048]{2,1,0:T(8,128)} %filt_hbm.1, ...), custom_call_target="tpu_custom_call" | custom-call | tf_op jit(solution)/shard_map/pallas_call | solution.py:436
  57.3 43.9 %shard_map.146 = bf16[192,2048]{1,0:T(8,128)(2,1)} custom-call(bf16[192,2048]{1,0:T(8,128)(2,1)} %tok_ref.3, f32[192,2048]{1,0:T(8,128)} %get-tuple-element.11.conv_ref, bf16[192,2048]{1,0:T(8,128)(2,1)} %get-tuple-element.12.norm_ref, f32[1,192]{1,0:T(1,128)} %bitcast.4, f32[1,192]{1,0:T(1,128)} %bitcast.5, bf16[192,192]{1,0:T(8,128)(2,1)} %get-tuple-element.13.mi_ref, ...), custom_call_target="tpu_custom_call" | custom-call | tf_op jit(solution)/shard_map/pallas_call | solution.py:551
  101.3 2.1 %copy.17 = bf16[192,2048]{1,0:T(8,128)(2,1)} copy(bf16[192,2048]{1,0:T(8,128)(2,1)} %shard_map.146) | data formatting | bytes 1572864
